TPU v7x, 256 devices: a whole 4x4x8 slice. The times are simulated.
256 devices in a mesh: row: 4 (over x), col: 4 (over z_lo), rep: 16 (over z_hi, y, core).
Axes of the slice: x: 4, y: 4, z: 8 (z_hi: 2, z_lo: 4; z = z_hi * 4 + z_lo), core: 2. Of those that a mesh axis runs over, the one named last changes fastest.
Arguments:
- integrals: bfloat16 [8192, 32768], P('row', ('col', 'rep')), may hold values from -0.0625 to 0.0625
- amplitudes: bfloat16 [32768, 4096], P(('row', 'rep'), 'col'), may hold values from -6 to 6
- tile_cols: int32 [64, 64], P('row'), may hold values from 0 to 255, as said below
Outputs:
- ladder: bfloat16 [8192, 4096], P(('row', 'rep'), 'col')
Inputs may be any that keep to these rules, and one draw needn't show every extreme that they name: `tile_cols`: tile columns are split into aligned groups of 4; entries g * 1 to (g + 1) - 1 of a tile row are 1 distinct tile columns of group g, in increasing order.
All inputs are finite; a program needn't handle non-finite values.
Results may differ from a plain program's by a relative error of at most 0.001.
Values may be sent and summed in bfloat16 or wider, within the bound.
A program may use at most 64 MiB of HBM per device.

v0:
```python
import jax
import jax.numpy as jnp
from jax import lax
from jax.sharding import PartitionSpec as P

TILE = 128


def screen_block(block, tile_cols, first_tile):
    row_count, width = block.shape
    ktiles = width // TILE
    wanted = first_tile + jnp.arange(ktiles, dtype=jnp.int32)
    matches = (tile_cols[:, :, None] == wanted[None, None, :]).astype(jnp.int32)
    keeper = (jnp.sum(matches, axis=1) > 0).astype(block.dtype)
    shaped = block.reshape(row_count // TILE, TILE, ktiles, TILE)
    return (shaped * keeper[:, None, :, None]).reshape(row_count, width)


def body(integrals, amplitudes, tile_cols):
    row_count, kdev_width = integrals.shape
    n_rep = lax.axis_size("rep")
    layer = lax.axis_index("rep")
    column = lax.axis_index("col")
    amp_rows = lax.all_gather(amplitudes, "row", axis=0, tiled=True)
    own = screen_block(integrals, tile_cols, (column * n_rep + layer) * kdev_width // TILE)
    partial_sum = jnp.dot(
        lax.all_gather(own, "col", axis=1, tiled=True), amp_rows, preferred_element_type=jnp.float32
    )
    summed = lax.psum_scatter(partial_sum, "rep", scatter_dimension=0, tiled=True)
    return summed.astype(jnp.bfloat16)


def solution(mesh):
    return jax.shard_map(
        body,
        mesh=mesh,
        in_specs=(P("row", ("col", "rep")), P(("row", "rep"), "col"), P("row", None)),
        out_specs=P(("row", "rep"), "col"),
        check_vma=False,
    )
```

profile of v0, /device:TPU:32, one launch (start us, length us, event | category | flops | bytes accessed | tf_op | source)
XLA Modules:
  0.0 382.8 jit_solution(4327294864894225420)
XLA Ops:
  6.5 0.0 copy-start
  6.5 0.0 all-gather.5.cloned.1.call-start
  6.5 0.7 all-gather.5.cloned.1.call-update
  7.3 0.0 all-gather.3.cloned.1.call-start
  7.3 0.9 convert_reduce_fusion
  8.3 0.1 copy.4
  8.4 0.6 mul.19
  9.0 0.0 copy-done
  9.0 1.6 bitcast_multiply_fusion
  10.6 0.0 all-gather.3.cloned.1.call-update
  10.6 0.0 reduce-scatter.2.cloned.1.call-start
  10.7 51.9 %all-gather.5.cloned.1.call-done = bf16[2048,1024]{1,0:T(8,128)(2,1)} async-done(((bf16[512,1024]{1,0:T(8,128)(2,1)}), bf16[2048,1024]{1,0:T(8,128)(2,1)}) %all-gather.5.cloned.1.call-update) | async-done | bytes 4194320 | tf_op jit(solution)/shard_map/all_gather | solution.py:24
  62.6 155.1 %all-gather.3.cloned.1.call-done = bf16[2048,2048]{1,0:T(8,128)(2,1)} async-done(((bf16[2048,512]{1,0:T(8,128)(2,1)}), bf16[2048,2048]{1,0:T(8,128)(2,1)}) %all-gather.3.cloned.1.call-update) | async-done | bytes 8388624 | tf_op jit(solution)/shard_map/all_gather | solution.py:27
  217.7 14.4 %fusion = f32[2048,1024]{1,0:T(8,128)} fusion(bf16[2048,2048]{1,0:T(8,128)(2,1)} %all-gather.3.cloned.1.call-done, bf16[2048,1024]{1,0:T(8,128)(2,1)} %all-gather.5.cloned.1.call-done), kind=kOutput, calls=%fused_computation.4 | convolution fusion | flops 8589934592 | bytes 20971520 | tf_op jit(solution)/shard_map/dot_general | solution.py:26
  232.1 0.0 reduce-scatter.2.cloned.1.call-update
  232.1 142.3 %reduce-scatter.2.cloned.1.call-done = f32[128,1024]{1,0:T(8,128)} async-done(((f32[2048,1024]{1,0:T(8,128)}), f32[128,1024]{1,0:T(8,128)}) %reduce-scatter.2.cloned.1.call-update) | async-done | bytes 524304 | tf_op jit(solution)/shard_map/reduce_scatter | solution.py:29
  374.5 1.8 convert_element_type.15
  (2 shorter events, 0.0 us)
Async XLA Ops:
  6.5 2.4 copy-start
  6.5 56.1 %all-gather.5.cloned.1.call-start = ((), (), s32[]{:S(2)}) async-start(), calls=%async_computation.2 | async-start | bytes 5242880 | tf_op jit(solution)/shard_map/all_gather | solution.py:24
  7.3 210.5 %all-gather.3.cloned.1.call-start = ((), (), s32[]{:S(2)}) async-start(), calls=%async_computation.1 | async-start | bytes 10485760 | tf_op jit(solution)/shard_map/all_gather | solution.py:27
  10.6 363.8 %reduce-scatter.2.cloned.1.call-start = ((), (), s32[]{:S(2)}) async-start(), calls=%async_computation.3 | async-start | bytes 8912896 | tf_op jit(solution)/shard_map/reduce_scatter | solution.py:29
Sparse Core Ops, SparseCore 0:
  9.2 53.3 all-gather.4
  64.4 153.2 all-gather.2
  232.3 142.1 reduce-scatter.1
where the time goes:
time: 384 us; the launch traced here: 383 us
  waiting for transfers between devices  350 us (91%)
  matrix products  14.4 us (4%)
  between operations  13.2 us (3%)
  other arithmetic  4.32 us (1%)
    all_gather x1, waiting for transfers between devices, body(): lax.all_gather(own, 'col', axis=1, tiled=True)  155 us
    reduce_scatter x1, waiting for transfers between devices, body(): lax.psum_scatter(partial_sum, 'rep', scatter_dimension=0, tiled=True)  142 us
    all_gather x1, waiting for transfers between devices, body(): amp_rows = lax.all_gather(amplitudes, 'row', axis=0, tiled=True)  51.9 us
    dot_general x1, matrix products, body(): jnp.dot(lax.all_gather(own, 'col', axis=1, tiled=True), amp_rows, preferr...  14.4 us
  transfers between devices with their start and end apart: 3, of which 3 were waited for; matrix products, arithmetic and copies ran while one was open for 1% of the time, Pallas kernels for 0%

commit v1 on v0

v1 whole, which is shorter than its diff:
```python
import jax
import jax.numpy as jnp
from jax import lax
from jax.experimental import pallas as pl
from jax.experimental.pallas import tpu as pltpu
from jax.sharding import PartitionSpec as P

TILE = 128
MESH = pl.DeviceIdType.MESH
BF16 = jnp.bfloat16
F32 = jnp.float32

NQ = 8
NC = 2 * NQ
AHEAD = 3
LAG_DOT = 2
LAG_CORE = 3
LAG_Y1 = 5
LAG_Y2 = 7


def choose(j, tiles):
    low = jnp.where(j == 0, tiles[0], tiles[1])
    high = jnp.where(j == 2, tiles[2], tiles[3])
    return jnp.where(j < 2, low, high)


def kernel(integrals, amplitudes, tile_cols, out,
           raw0, raw1, ints, a0, a1, a2, a3, a4, a5, a6, a7, keep, give, got, y1, y2, zgot,
           load_a, load_i, a_send, a_recv, af_send, af_recv,
           i_send, i_recv, if_send, c_send, c_recv,
           y1_send, y1_recv, y2_send, y2_recv, z_send, z_recv):
    x = lax.axis_index("row")
    zl = lax.axis_index("col")
    p = lax.axis_index("rep")
    zh = p // 8
    y = lax.rem(p // 2, 4)
    core = lax.rem(p, 2)
    z = zh * 4 + zl
    xr, xl = lax.rem(x + 1, 4), lax.rem(x + 3, 4)
    yr, yl, yo = lax.rem(y + 1, 4), lax.rem(y + 3, 4), lax.rem(y + 2, 4)

    def at_x(v):
        return (v, zl, p)

    def at_y(v):
        return (x, zl, zh * 8 + v * 2 + core)

    def at_z(v):
        v = lax.rem(v + 8, 8)
        return (x, lax.rem(v, 4), (v // 4) * 8 + y * 2 + core)

    other_core = (x, zl, zh * 8 + y * 2 + (1 - core))

    def remote(src, dst, send, recv, dev):
        return pltpu.make_async_remote_copy(
            src_ref=src, dst_ref=dst, send_sem=send, recv_sem=recv,
            device_id=dev, device_id_type=MESH)

    def half(m):
        return (1 - zh) * (1 - m) + zh * m

    raw = (raw0, raw1)
    amps = (a0, a1, a2, a3, a4, a5, a6, a7)

    def i_load(m):
        rows = pl.ds(pl.multiple_of(half(m) * 1024, 1024), 1024)
        return pltpu.make_async_copy(integrals.at[rows], raw[m], load_i.at[m])

    for m in range(2):
        i_load(m).start()

    def a_load(q):
        cols = pl.ds(pl.multiple_of(q * TILE, TILE), TILE)
        return pltpu.make_async_copy(amplitudes.at[:, cols], amps[q].at[x], load_a.at[q])

    for q in range(NQ):
        a_load(q).start()

    barrier = pltpu.get_barrier_semaphore()
    partners = [at_x(xr), at_x(xl), at_y(yr), at_y(yl), at_z(z + 1), at_z(z - 1),
                at_z(z + 2), at_z(z - 2), at_z(z + 4), other_core]
    for dev in partners:
        pl.semaphore_signal(barrier, inc=1, device_id=dev, device_id_type=MESH)

    def pack(m):
        i_load(m).wait()
        group = zl * 16 + p
        for k in range(8):
            i = half(m) * 8 + k
            j = tile_cols[i, group] - group * 4
            rows = pl.ds(k * TILE, TILE)
            ints[zl, i] = choose(j, [raw[m][rows, pl.ds(n * TILE, TILE)] for n in range(4)])

    def i_copy(m, h, send, target):
        part = ints.at[h, pl.ds(half(m) * 8, 8)]
        return remote(part, part, send, i_recv.at[m, h], at_z(zh * 4 + target))

    steps = ((0, 2), (1, -2), (2, 1), (3, -1))

    def i_own(m, wait):
        for s, d in steps:
            @pl.when((zl + d >= 0) & (zl + d < 4))
            def _():
                copy = i_copy(m, zl, i_send.at[m, s], zl + d)
                if wait:
                    copy.wait_send()
                else:
                    copy.start()

    def i_forward(m, wait):
        @pl.when((zl == 1) | (zl == 2))
        def _():
            h = jnp.where(zl == 2, 0, 3)
            copy = i_copy(m, h, if_send.at[m], jnp.where(zl == 2, 3, 0))
            if wait:
                copy.wait_send()
            else:
                copy.wait_recv()
                copy.start()

    def i_arrive(m):
        for d in range(1, 4):
            h = lax.rem(zl + d, 4)

            @pl.when(jnp.logical_not(((zl == 2) & (h == 0)) | ((zl == 1) & (h == 3))))
            def _():
                i_copy(m, h, if_send.at[m], zl).wait_recv()

    def a_own(q, d):
        part = amps[q].at[x]
        return remote(part, part, a_send.at[q, d], a_recv.at[q, d], at_x((xr, xl)[d]))

    def a_from(q, d):
        part = amps[q].at[(xl, xr)[d]]
        return remote(part, part, a_send.at[q, d], a_recv.at[q, d], at_x((xr, xl)[d]))

    def a_pass(q, d):
        part = amps[q].at[(xl, xr)[d], pl.ds(d * 256, 256)]
        return remote(part, part, af_send.at[q, d], af_recv.at[q, d], at_x((xr, xl)[d]))

    def a_passed(q, d):
        part = amps[q].at[lax.rem(x + 2, 4), pl.ds(d * 256, 256)]
        return remote(part, part, af_send.at[q, d], af_recv.at[q, d], at_x((xr, xl)[d]))

    def a_start(q):
        a_load(q).wait()
        for d in range(2):
            a_own(q, d).start()

    pack(0)
    pl.semaphore_wait(barrier, len(partners))
    i_own(0, False)
    for q in range(AHEAD):
        a_start(q)
    pack(1)
    i_own(1, False)

    def product(c, m, q, cc, dst):
        def row(yy, carry):
            i = half(m) * 8 + yy * 2 + cc
            lhs, rhs = [], []
            for h in range(4):
                group = h * 16 + p
                j = tile_cols[i, group] - group * 4
                lhs.append(ints[h, i])
                rhs.append(choose(j, [amps[q][h, pl.ds(n * TILE, TILE)] for n in range(4)]))
            dst[c, yy] = jnp.dot(jnp.concatenate(lhs, axis=1), jnp.concatenate(rhs, axis=0),
                                 preferred_element_type=F32)
            return carry
        lax.fori_loop(0, 4, row, 0)

    def core_copy(c):
        return remote(give.at[c], got.at[c], c_send, c_recv.at[c], other_core)

    def y1_copy(c, d):
        return remote(keep.at[c, yo, pl.ds(d * 64, 64)], y1.at[c, d], y1_send, y1_recv.at[c, d],
                      at_y((yr, yl)[d]))

    def y2_copy(c, d):
        return remote(keep.at[c, (yr, yl)[d]], y2.at[c, d], y2_send, y2_recv.at[c, d],
                      at_y((yr, yl)[d]))

    def z_copy(q):
        return remote(keep.at[q, y], zgot.at[q], z_send, z_recv.at[q], at_z(z + 4))

    def tick(t, carry):
        for q in range(NQ):
            @pl.when(t == q)
            def _():
                for d in range(2):
                    a_from(q, d).wait_recv()
                    a_pass(q, d).start()
                if q + AHEAD < NQ:
                    a_start(q + AHEAD)

        @pl.when(t == 1)
        def _():
            i_forward(0, False)

        @pl.when(t == 4)
        def _():
            i_forward(1, False)

        c = t - LAG_DOT

        @pl.when(c == 0)
        def _():
            i_arrive(0)

        @pl.when(c == NQ)
        def _():
            i_arrive(1)

        m = c // NQ
        for q in range(NQ):
            @pl.when(c == q)
            def _():
                for d in range(2):
                    a_passed(q, d).wait_recv()

            @pl.when((c == q) | (c == q + NQ))
            def _():
                product(c, m, q, 1 - core, give)
                core_copy(c).start()
                product(c, m, q, core, keep)

        c1 = t - LAG_CORE

        @pl.when((c1 >= 0) & (c1 < NC))
        def _():
            core_copy(c1).wait_recv()
            keep[c1, yo] += got[c1, yo]
            for d in range(2):
                y1_copy(c1, d).start()
            for v in (yr, yl, y):
                keep[c1, v] += got[c1, v]

        c2 = t - LAG_Y1

        @pl.when((c2 >= 0) & (c2 < NC))
        def _():
            for d in range(2):
                y1_copy(c2, d).wait_recv()
                keep[c2, (yr, yl)[d], pl.ds(d * 64, 64)] += y1[c2, d]
                y2_copy(c2, d).start()

        c3 = t - LAG_Y2

        @pl.when((c3 >= 0) & (c3 < NC))
        def _():
            for d in range(2):
                y2_copy(c3, d).wait_recv()

            @pl.when(c3 < NQ)
            def _():
                keep[c3, y] += y2[c3, 0] + y2[c3, 1]
                z_copy(c3).start()

            @pl.when(c3 >= NQ)
            def _():
                q = c3 - NQ
                z_copy(q).wait_recv()
                total = (keep[c3, y] + y2[c3, 0]) + (y2[c3, 1] + zgot[q])
                out[:, pl.ds(pl.multiple_of(q * TILE, TILE), TILE)] = total.astype(BF16)

        return carry

    lax.fori_loop(0, NC + LAG_Y2, tick, 0)

    for m in range(2):
        i_own(m, True)
        i_forward(m, True)
    for d in range(2):
        for q in range(NQ):
            a_own(q, d).wait_send()
            a_pass(q, d).wait_send()
    for buf, sem in ((give, c_send), (y1, y1_send), (y2, y2_send), (zgot, z_send)):
        remote(buf, buf, sem, c_recv.at[0], other_core).wait_send()


def body(integrals, amplitudes, tile_cols):
    dma = pltpu.SemaphoreType.DMA
    return pl.pallas_call(
        kernel,
        out_shape=jax.ShapeDtypeStruct((TILE, 1024), BF16),
        in_specs=[pl.BlockSpec(memory_space=pl.ANY), pl.BlockSpec(memory_space=pl.ANY),
                  pl.BlockSpec(memory_space=pltpu.SMEM)],
        out_specs=pl.BlockSpec(memory_space=pltpu.VMEM),
        scratch_shapes=[
            *[pltpu.VMEM((1024, 512), BF16)] * 2,
            pltpu.VMEM((4, 16, TILE, TILE), BF16),
            *[pltpu.VMEM((4, 512, TILE), BF16)] * NQ,
            pltpu.VMEM((NC, 4, TILE, TILE), F32),
            pltpu.VMEM((NC, 4, TILE, TILE), F32),
            pltpu.VMEM((NC, 4, TILE, TILE), F32),
            pltpu.VMEM((NC, 2, 64, TILE), F32),
            pltpu.VMEM((NC, 2, TILE, TILE), F32),
            pltpu.VMEM((NQ, TILE, TILE), F32),
            dma((NQ,)), dma((2,)), *[dma((NQ, 2))] * 4,
            dma((2, 4)), dma((2, 4)), dma((2,)), dma, dma((NC,)),
            dma, dma((NC, 2)), dma, dma((NC, 2)), dma, dma((NQ,)),
        ],
        compiler_params=pltpu.CompilerParams(
            collective_id=0, has_side_effects=True, vmem_limit_bytes=48 << 20),
        cost_estimate=pl.CostEstimate(flops=2 << 30, bytes_accessed=4 << 20, transcendentals=0),
    )(integrals, amplitudes, tile_cols)


def solution(mesh):
    return jax.shard_map(
        body,
        mesh=mesh,
        in_specs=(P("row", ("col", "rep")), P(("row", "rep"), "col"), P("row", None)),
        out_specs=P(("row", "rep"), "col"),
        check_vma=False,
    )
```

time: 384 us -> 91 us (0.24)
  waiting for transfers between devices: 350 us -> 0 us
  Pallas kernels: 0 us -> 86.6 us
  matrix products: 14.4 us -> 0 us
  between operations: 13.2 us -> 0.01 us
  other arithmetic: 4.32 us -> 0 us
    all_gather x2 -> x0, waiting for transfers between devices: 207 us -> none  [the longest x1 155 us: body(): lax.all_gather(own, 'col', axis=1, tiled=True)]
    reduce_scatter x1 -> x0, waiting for transfers between devices: 142 us -> none  [body(): lax.psum_scatter(partial_sum, 'rep', scatter_dimension=0, tiled=True)]
    pallas_call x0 -> x1, Pallas kernels: none -> 86.6 us  [body(): pl.pallas_call(kernel, out_shape=jax.ShapeDtypeStruct((TILE, 1024), BF16)...]
    dot_general x1 -> x0, matrix products: 14.4 us -> none  [body(): jnp.dot(lax.all_gather(own, 'col', axis=1, tiled=True), amp_rows, preferr...]
    unnamed x2 -> x7, local copies, waits for them, and re-layouts: 0.01 us -> 4.22 us
  transfers between devices with their start and end apart: 3 -> 0, of which waited for: 3 -> 0; matrix products, arithmetic and copies ran while one was open for 1% -> 0% of each run, Pallas kernels for 0% -> 0%
where the time goes in v1:
time: 91 us; the launch traced here: 90.8 us
  Pallas kernels  86.6 us (95%)
  local copies, waits for them, and re-layouts  4.22 us (5%)
    pallas_call x1, Pallas kernels, body(): pl.pallas_call(kernel, out_shape=jax.ShapeDtypeStruct((TILE, 1024), BF16)...  86.6 us
    unnamed x7, local copies, waits for them, and re-layouts  4.22 us

profile of v1, /device:TPU:32, one launch (start us, length us, event | category | flops | bytes accessed | tf_op | source)
XLA Modules:
  0.0 90.8 jit_solution(15421944667238374998)
XLA Ops:
  0.0 0.0 copy-start
  0.0 1.6 %copy-done = bf16[2048,512]{1,0:T(8,128)(2,1)S(1)} copy-done((bf16[2048,512]{1,0:T(8,128)(2,1)S(1)}, bf16[2048,512]{1,0:T(8,128)(2,1)}, u32[]{:S(2)}) %copy-start) | copy-done | bytes 2097176
  1.6 0.0 copy-start.1
  1.6 1.2 %copy-done.1 = bf16[512,1024]{1,0:T(8,128)(2,1)S(1)} copy-done((bf16[512,1024]{1,0:T(8,128)(2,1)S(1)}, bf16[512,1024]{1,0:T(8,128)(2,1)}, u32[]{:S(2)}) %copy-start.1) | copy-done | bytes 1048600
  2.8 0.0 copy-start.2
  2.8 0.7 copy-done.2
  3.5 86.6 %shard_map.37 = bf16[128,1024]{1,0:T(8,128)(2,1)S(1)} custom-call(bf16[2048,512]{1,0:T(8,128)(2,1)S(1)} %copy-done, bf16[512,1024]{1,0:T(8,128)(2,1)S(1)} %copy-done.1, s32[16,64]{1,0:T(8,128)S(1)} %copy-done.2), custom_call_target="tpu_custom_call" | custom-call | flops 2147483648 | bytes 4194304 | tf_op jit(solution)/shard_map/pallas_call | solution.py:284
  90.1 0.7 copy.5
Async XLA Ops:
  0.0 1.6 %copy-start = (bf16[2048,512]{1,0:T(8,128)(2,1)S(1)}, bf16[2048,512]{1,0:T(8,128)(2,1)}, u32[]{:S(2)}) copy-start(bf16[2048,512]{1,0:T(8,128)(2,1)} %integrals.1) | copy-start | bytes 6291460
  1.6 1.2 %copy-start.1 = (bf16[512,1024]{1,0:T(8,128)(2,1)S(1)}, bf16[512,1024]{1,0:T(8,128)(2,1)}, u32[]{:S(2)}) copy-start(bf16[512,1024]{1,0:T(8,128)(2,1)} %amplitudes.1) | copy-start | bytes 3145732
  2.8 0.7 copy-start.2

commit v2 on v1

v2 whole, which is shorter than its diff:
```python
import jax
import jax.numpy as jnp
from jax import lax
from jax.experimental import pallas as pl
from jax.experimental.pallas import tpu as pltpu
from jax.sharding import PartitionSpec as P

TILE = 128
MESH = pl.DeviceIdType.MESH
BF16 = jnp.bfloat16
F32 = jnp.float32

NQ = 8
HALF = 64
WIDE = 256
ORDER = ((0, 0), (0, 1), (1, 0), (1, 1), (2, 0), (2, 1), (0, 2), (1, 2),
         (2, 2), (0, 3), (1, 3), (2, 3), (3, 0), (3, 1), (3, 2), (3, 3))
NC = len(ORDER)
A_TICK = (0, 1, 2, 3, 5, 6, 9, 11)
I_TICK = (1, 4, 7, 10)
C_TICK = (4, 7, 8, 9, 10, 11, 12, 13, 14, 15, 16, 17, 18, 19, 20, 21)
AHEAD = 3
LAG_CORE = 1
LAG_Y1 = 3
LAG_Y2 = 5


def choose(j, tiles):
    low = jnp.where(j == 0, tiles[0], tiles[1])
    high = jnp.where(j == 2, tiles[2], tiles[3])
    return jnp.where(j < 2, low, high)


def kernel(integrals, amplitudes, cols_in, out,
           tile_cols, raw0, raw1, ints, a0, a1, a2, a3, a4, a5, a6, a7, keep, give, got, y1, y2, zgot,
           load_t, load_a, load_i, a_send, a_recv, af_send, af_recv,
           i_send, i_recv, if_send, c_send, c_recv,
           y1_send, y1_recv, y2_send, y2_recv, z_send, z_recv):
    x = lax.axis_index("row")
    zl = lax.axis_index("col")
    p = lax.axis_index("rep")
    zh = p // 8
    y = lax.rem(p // 2, 4)
    core = lax.rem(p, 2)
    z = zh * 4 + zl
    xr, xl = lax.rem(x + 1, 4), lax.rem(x + 3, 4)
    yr, yl, yo = lax.rem(y + 1, 4), lax.rem(y + 3, 4), lax.rem(y + 2, 4)

    def at_x(v):
        return (v, zl, p)

    def at_y(v):
        return (x, zl, zh * 8 + v * 2 + core)

    def at_z(v):
        v = lax.rem(v + 8, 8)
        return (x, lax.rem(v, 4), (v // 4) * 8 + y * 2 + core)

    other_core = (x, zl, zh * 8 + y * 2 + (1 - core))

    def remote(src, dst, send, recv, dev):
        return pltpu.make_async_remote_copy(
            src_ref=src, dst_ref=dst, send_sem=send, recv_sem=recv,
            device_id=dev, device_id_type=MESH)

    def half(m):
        return (1 - zh) * (1 - m) + zh * m

    raw = (raw0, raw1)
    amps = (a0, a1, a2, a3, a4, a5, a6, a7)

    def i_load(m):
        rows = pl.ds(pl.multiple_of(half(m) * 1024, 1024), 1024)
        return pltpu.make_async_copy(integrals.at[rows], raw[m], load_i.at[m])

    t_load = pltpu.make_async_copy(cols_in, tile_cols, load_t)
    t_load.start()
    for m in range(2):
        i_load(m).start()

    def a_load(q):
        cols = pl.ds(pl.multiple_of(q * TILE, TILE), TILE)
        return pltpu.make_async_copy(amplitudes.at[:, cols], amps[q].at[x], load_a.at[q])

    for q in range(NQ):
        a_load(q).start()

    barrier = pltpu.get_barrier_semaphore()
    partners = [at_x(xr), at_x(xl), at_y(yr), at_y(yl), at_z(z + 1), at_z(z - 1),
                at_z(z + 2), at_z(z - 2), at_z(z + 4), other_core]
    for dev in partners:
        pl.semaphore_signal(barrier, inc=1, device_id=dev, device_id_type=MESH)

    def pack(m):
        i_load(m).wait()
        group = zl * 16 + p
        for k in range(8):
            i = half(m) * 8 + k
            j = tile_cols[i, group] - group * 4
            rows = pl.ds(k * TILE, TILE)
            ints[zl, i] = choose(j, [raw[m][rows, pl.ds(n * TILE, TILE)] for n in range(4)])

    def i_copy(u, h, send, target):
        part = ints.at[h, pl.ds(half(u // 2) * 8, 8), pl.ds(u % 2 * HALF, HALF)]
        return remote(part, part, send, i_recv.at[u, h], at_z(zh * 4 + target))

    steps = ((0, 2), (1, -2), (2, 1), (3, -1))

    def i_own(u, wait):
        for s, d in steps:
            @pl.when((zl + d >= 0) & (zl + d < 4))
            def _():
                copy = i_copy(u, zl, i_send.at[u, s], zl + d)
                if wait:
                    copy.wait_send()
                else:
                    copy.start()

    def i_forward(u, wait):
        @pl.when((zl == 1) | (zl == 2))
        def _():
            h = jnp.where(zl == 2, 0, 3)
            copy = i_copy(u, h, if_send.at[u], jnp.where(zl == 2, 3, 0))
            if wait:
                copy.wait_send()
            else:
                copy.wait_recv()
                copy.start()

    def i_arrive(u):
        for d in range(1, 4):
            h = lax.rem(zl + d, 4)

            @pl.when(jnp.logical_not(((zl == 2) & (h == 0)) | ((zl == 1) & (h == 3))))
            def _():
                i_copy(u, h, if_send.at[u], zl).wait_recv()

    def a_own(q, d):
        part = amps[q].at[x]
        return remote(part, part, a_send.at[q, d], a_recv.at[q, d], at_x((xr, xl)[d]))

    def a_from(q, d):
        part = amps[q].at[(xl, xr)[d]]
        return remote(part, part, a_send.at[q, d], a_recv.at[q, d], at_x((xr, xl)[d]))

    def a_pass(q, d):
        part = amps[q].at[(xl, xr)[d], pl.ds(d * 256, 256)]
        return remote(part, part, af_send.at[q, d], af_recv.at[q, d], at_x((xr, xl)[d]))

    def a_passed(q, d):
        part = amps[q].at[lax.rem(x + 2, 4), pl.ds(d * 256, 256)]
        return remote(part, part, af_send.at[q, d], af_recv.at[q, d], at_x((xr, xl)[d]))

    def a_start(q):
        a_load(q).wait()
        for d in range(2):
            a_own(q, d).start()

    t_load.wait()
    pack(0)
    pl.semaphore_wait(barrier, len(partners))
    i_own(0, False)
    for q in range(AHEAD):
        a_start(q)
    i_own(1, False)
    pack(1)

    def product(c, u, pair, cc, dst):
        for yy in range(4):
            i = half(u // 2) * 8 + yy * 2 + cc
            rows = pl.ds(pl.multiple_of(lax.rem(u, 2) * HALF, HALF), HALF)
            lhs, rhs = [], []
            for h in range(4):
                group = h * 16 + p
                j = tile_cols[i, group] - group * 4
                lhs.append(ints[h, i, rows])
                rhs.append(jnp.concatenate(
                    [choose(j, [amps[q][h, pl.ds(n * TILE, TILE)] for n in range(4)])
                     for q in (pair * 2, pair * 2 + 1)], axis=1))
            dst[c, yy] = jnp.dot(jnp.concatenate(lhs, axis=1), jnp.concatenate(rhs, axis=0),
                                 preferred_element_type=F32)

    def core_copy(c):
        return remote(give.at[c], got.at[c], c_send, c_recv.at[c], other_core)

    def y1_copy(c, d):
        return remote(keep.at[c, yo, pl.ds(d * 32, 32)], y1.at[c, d], y1_send, y1_recv.at[c, d],
                      at_y((yr, yl)[d]))

    def y2_copy(c, d):
        return remote(keep.at[c, (yr, yl)[d]], y2.at[c, d], y2_send, y2_recv.at[c, d],
                      at_y((yr, yl)[d]))

    def z_copy(c, u, pair):
        return remote(keep.at[c, y], zgot.at[lax.rem(u, 2), pair], z_send,
                      z_recv.at[lax.rem(u, 2), pair], at_z(z + 4))

    def table(t, ticks, values, none):
        found = jnp.int32(none)
        for at, value in zip(ticks, values):
            found = jnp.where(t == at, value, found)
        return found

    def tick(t, carry):
        for q in range(NQ):
            @pl.when(t == A_TICK[q])
            def _():
                for d in range(2):
                    a_from(q, d).wait_recv()
                    a_pass(q, d).start()
                if q + AHEAD < NQ:
                    a_start(q + AHEAD)

        for u in range(4):
            @pl.when(t == I_TICK[u])
            def _():
                i_forward(u, False)
                if u + 2 < 4:
                    i_own(u + 2, False)

        c = table(t, C_TICK, range(NC), -1)
        pair = table(t, C_TICK, [o[1] for o in ORDER], -1)
        u = table(t, C_TICK, [o[0] for o in ORDER], 0)
        for w in range(4):
            @pl.when(t == C_TICK[ORDER.index((w, 0))])
            def _():
                i_arrive(w)

            @pl.when(t == C_TICK[ORDER.index((0, w))])
            def _():
                for q in (w * 2, w * 2 + 1):
                    for d in range(2):
                        a_passed(q, d).wait_recv()

        for w in range(4):
            @pl.when(pair == w)
            def _():
                product(c, u, w, 1 - core, give)
                core_copy(c).start()
                product(c, u, w, core, keep)

        c1 = table(t - LAG_CORE, C_TICK, range(NC), -1)

        @pl.when(c1 >= 0)
        def _():
            core_copy(c1).wait_recv()
            keep[c1, yo] += got[c1, yo]
            for d in range(2):
                y1_copy(c1, d).start()
            for v in (yr, yl, y):
                keep[c1, v] += got[c1, v]

        c2 = table(t - LAG_Y1, C_TICK, range(NC), -1)

        @pl.when(c2 >= 0)
        def _():
            for d in range(2):
                y1_copy(c2, d).wait_recv()
                keep[c2, (yr, yl)[d], pl.ds(d * 32, 32)] += y1[c2, d]
                y2_copy(c2, d).start()

        c3 = table(t - LAG_Y2, C_TICK, range(NC), -1)
        pair3 = table(t - LAG_Y2, C_TICK, [o[1] for o in ORDER], 0)
        u3 = table(t - LAG_Y2, C_TICK, [o[0] for o in ORDER], 0)

        @pl.when(c3 >= 0)
        def _():
            for d in range(2):
                y2_copy(c3, d).wait_recv()

            @pl.when(u3 < 2)
            def _():
                keep[c3, y] += y2[c3, 0] + y2[c3, 1]
                z_copy(c3, u3, pair3).start()

            @pl.when(u3 >= 2)
            def _():
                z_copy(c3, u3, pair3).wait_recv()
                total = (keep[c3, y] + y2[c3, 0]) + (y2[c3, 1] + zgot[u3 - 2, pair3])
                out[pl.ds(pl.multiple_of((u3 - 2) * HALF, HALF), HALF),
                    pl.ds(pl.multiple_of(pair3 * WIDE, WIDE), WIDE)] = total.astype(BF16)

        return carry

    lax.fori_loop(0, C_TICK[-1] + LAG_Y2 + 1, tick, 0)

    for u in range(4):
        i_own(u, True)
        i_forward(u, True)
    for d in range(2):
        for q in range(NQ):
            a_own(q, d).wait_send()
            a_pass(q, d).wait_send()
    for buf, sem in ((give, c_send), (y1, y1_send), (y2, y2_send), (zgot, z_send)):
        remote(buf, buf, sem, c_recv.at[0], other_core).wait_send()


def body(integrals, amplitudes, tile_cols):
    dma = pltpu.SemaphoreType.DMA
    return pl.pallas_call(
        kernel,
        out_shape=jax.ShapeDtypeStruct((TILE, 1024), BF16),
        in_specs=[pl.BlockSpec(memory_space=pltpu.HBM)] * 3,
        out_specs=pl.BlockSpec(memory_space=pltpu.VMEM),
        scratch_shapes=[
            pltpu.SMEM((16, 64), jnp.int32),
            *[pltpu.VMEM((1024, 512), BF16)] * 2,
            pltpu.VMEM((4, 16, TILE, TILE), BF16),
            *[pltpu.VMEM((4, 512, TILE), BF16)] * NQ,
            *[pltpu.VMEM((NC, 4, HALF, WIDE), F32)] * 3,
            pltpu.VMEM((NC, 2, HALF // 2, WIDE), F32),
            pltpu.VMEM((NC, 2, HALF, WIDE), F32),
            pltpu.VMEM((2, 4, HALF, WIDE), F32),
            dma, dma((NQ,)), dma((2,)), *[dma((NQ, 2))] * 4,
            dma((4, 4)), dma((4, 4)), dma((4,)), dma, dma((NC,)),
            dma, dma((NC, 2)), dma, dma((NC, 2)), dma, dma((2, 4)),
        ],
        compiler_params=pltpu.CompilerParams(
            collective_id=0, has_side_effects=True, vmem_limit_bytes=60 << 20),
        cost_estimate=pl.CostEstimate(flops=2 << 30, bytes_accessed=4 << 20, transcendentals=0),
    )(integrals, amplitudes, tile_cols)


def solution(mesh):
    return jax.shard_map(
        body,
        mesh=mesh,
        in_specs=(P("row", ("col", "rep")), P(("row", "rep"), "col"), P("row", None)),
        out_specs=P(("row", "rep"), "col"),
        check_vma=False,
    )
```

time: 91 us -> 80.9 us (0.89); the launches traced: 90.8 us -> 79.4 us
  Pallas kernels: 86.6 us -> 77.7 us
  local copies, waits for them, and re-layouts: 4.22 us -> 1.67 us
    pallas_call x1, Pallas kernels: 86.6 us -> 77.7 us  [body(): pl.pallas_call(kernel, out_shape=jax.ShapeDtypeStruct((TILE, 1024), BF16)...]
    unnamed x7 -> x1, local copies, waits for them, and re-layouts: 4.22 us -> 1.67 us
where the time goes in v2:
time: 80.9 us; the launch traced here: 79.4 us
  Pallas kernels  77.7 us (96%)
  local copies, waits for them, and re-layouts  1.67 us (2%)
    pallas_call x1, Pallas kernels, body(): pl.pallas_call(kernel, out_shape=jax.ShapeDtypeStruct((TILE, 1024), BF16)...  77.7 us
    unnamed x1, local copies, waits for them, and re-layouts  1.67 us

profile of v2, /device:TPU:32, one launch (start us, length us, event | category | flops | bytes accessed | tf_op | source)
XLA Modules:
  0.0 79.4 jit_solution(2583729358254232575)
XLA Ops:
  0.0 77.7 %shard_map.37 = bf16[128,1024]{1,0:T(8,128)(2,1)} custom-call(bf16[2048,512]{1,0:T(8,128)(2,1)} %integrals.1, bf16[512,1024]{1,0:T(8,128)(2,1)} %amplitudes.1, s32[16,64]{1,0:T(8,128)} %cols_in.1), custom_call_target="tpu_custom_call" | custom-call | flops 2147483648 | bytes 4194304 | tf_op jit(solution)/shard_map/pallas_call | solution.py:300
  77.7 1.7 %copy.5 = bf16[128,1024]{1,0:T(8,128)(2,1)} copy(bf16[128,1024]{1,0:T(8,128)(2,1)} %shard_map.37) | data formatting | bytes 524288

commit v3 on v2

--- a/solution.py
+++ b/solution.py
@@ -13,16 +13,17 @@
 NQ = 8
 HALF = 64
 WIDE = 256
-ORDER = ((0, 0), (0, 1), (1, 0), (1, 1), (2, 0), (2, 1), (0, 2), (1, 2),
-         (2, 2), (0, 3), (1, 3), (2, 3), (3, 0), (3, 1), (3, 2), (3, 3))
+ORDER = ((0, 0), (1, 0), (0, 1), (1, 1), (2, 0), (2, 1), (0, 2), (1, 2),
+         (0, 3), (1, 3), (2, 2), (2, 3), (3, 0), (3, 1), (3, 2), (3, 3))
 NC = len(ORDER)
-A_TICK = (0, 1, 2, 3, 5, 6, 9, 11)
-I_TICK = (1, 4, 7, 10)
-C_TICK = (4, 7, 8, 9, 10, 11, 12, 13, 14, 15, 16, 17, 18, 19, 20, 21)
+A_TICK = (2, 3, 5, 7, 9, 11, 13, 15)
+I_TICK = (4, 8, 11, 14)
+C_TICK = (8, 10, 12, 13, 14, 15, 16, 17,
+         18, 19, 20, 21, 22, 23, 24, 25)
 AHEAD = 3
 LAG_CORE = 1
-LAG_Y1 = 3
-LAG_Y2 = 5
+LAG_Y1 = 4
+LAG_Y2 = 8
 
 
 def choose(j, tiles):
@@ -222,11 +223,11 @@
         pair = table(t, C_TICK, [o[1] for o in ORDER], -1)
         u = table(t, C_TICK, [o[0] for o in ORDER], 0)
         for w in range(4):
-            @pl.when(t == C_TICK[ORDER.index((w, 0))])
+            @pl.when(t == C_TICK[min(i for i, o in enumerate(ORDER) if o[0] == w)])
             def _():
                 i_arrive(w)
 
-            @pl.when(t == C_TICK[ORDER.index((0, w))])
+            @pl.when(t == C_TICK[min(i for i, o in enumerate(ORDER) if o[1] == w)])
             def _():
                 for q in (w * 2, w * 2 + 1):
                     for d in range(2):

time: 80.9 us -> 79.1 us (0.978); the launches traced: 79.4 us -> 78.8 us
  no operation moved by 1% of the time
where the time goes in v3:
time: 79.1 us; the launch traced here: 78.8 us
  Pallas kernels  77.1 us (97%)
  local copies, waits for them, and re-layouts  1.67 us (2%)
    pallas_call x1, Pallas kernels, body(): pl.pallas_call(kernel, out_shape=jax.ShapeDtypeStruct((TILE, 1024), BF16)...  77.1 us
    unnamed x1, local copies, waits for them, and re-layouts  1.67 us

profile of v3, /device:TPU:32, one launch (start us, length us, event | category | flops | bytes accessed | tf_op | source)
XLA Modules:
  0.0 78.8 jit_solution(12505538999127700399)
XLA Ops:
  0.0 77.1 %shard_map.37 = bf16[128,1024]{1,0:T(8,128)(2,1)} custom-call(bf16[2048,512]{1,0:T(8,128)(2,1)} %integrals.1, bf16[512,1024]{1,0:T(8,128)(2,1)} %amplitudes.1, s32[16,64]{1,0:T(8,128)} %cols_in.1), custom_call_target="tpu_custom_call" | custom-call | flops 2147483648 | bytes 4194304 | tf_op jit(solution)/shard_map/pallas_call | solution.py:301
  77.1 1.7 %copy.5 = bf16[128,1024]{1,0:T(8,128)(2,1)} copy(bf16[128,1024]{1,0:T(8,128)(2,1)} %shard_map.37) | data formatting | bytes 524288

commit v4 on v3

--- a/solution.py
+++ b/solution.py
@@ -157,11 +157,12 @@
         for d in range(2):
             a_own(q, d).start()
 
+    pl.semaphore_wait(barrier, len(partners))
+    a_start(0)
     t_load.wait()
     pack(0)
-    pl.semaphore_wait(barrier, len(partners))
     i_own(0, False)
-    for q in range(AHEAD):
+    for q in range(1, AHEAD):
         a_start(q)
     i_own(1, False)
     pack(1)
@@ -317,7 +318,7 @@
             dma, dma((NC, 2)), dma, dma((NC, 2)), dma, dma((2, 4)),
         ],
         compiler_params=pltpu.CompilerParams(
-            collective_id=0, has_side_effects=True, vmem_limit_bytes=60 << 20),
+            collective_id=0, has_side_effects=True, vmem_limit_bytes=53 << 20),
         cost_estimate=pl.CostEstimate(flops=2 << 30, bytes_accessed=4 << 20, transcendentals=0),
     )(integrals, amplitudes, tile_cols)
 

time: 79.1 us -> 78.1 us (0.987)
    unnamed x1 -> x3, local copies, waits for them, and re-layouts: 1.67 us -> 1.4 us
where the time goes in v4:
time: 78.1 us; the launch traced here: 77.8 us
  Pallas kernels  76.4 us (98%)
  local copies, waits for them, and re-layouts  1.4 us (2%)
    pallas_call x1, Pallas kernels, body(): pl.pallas_call(kernel, out_shape=jax.ShapeDtypeStruct((TILE, 1024), BF16)...  76.4 us

profile of v4, /device:TPU:32, one launch (start us, length us, event | category | flops | bytes accessed | tf_op | source)
XLA Modules:
  0.0 77.8 jit_solution(16609059392233776877)
XLA Ops:
  0.0 0.0 copy-start
  0.0 0.7 copy-done
  0.7 76.4 %shard_map.37 = bf16[128,1024]{1,0:T(8,128)(2,1)S(1)} custom-call(bf16[2048,512]{1,0:T(8,128)(2,1)} %integrals.1, bf16[512,1024]{1,0:T(8,128)(2,1)} %amplitudes.1, s32[16,64]{1,0:T(8,128)S(1)} %copy-done), custom_call_target="tpu_custom_call" | custom-call | flops 2147483648 | bytes 4194304 | tf_op jit(solution)/shard_map/pallas_call | solution.py:302
  77.1 0.7 copy.5
Async XLA Ops:
  0.0 0.7 copy-start

commit v5 on v4

--- a/solution.py
+++ b/solution.py
@@ -16,10 +16,9 @@
 ORDER = ((0, 0), (1, 0), (0, 1), (1, 1), (2, 0), (2, 1), (0, 2), (1, 2),
          (0, 3), (1, 3), (2, 2), (2, 3), (3, 0), (3, 1), (3, 2), (3, 3))
 NC = len(ORDER)
-A_TICK = (2, 3, 5, 7, 9, 11, 13, 15)
-I_TICK = (4, 8, 11, 14)
-C_TICK = (8, 10, 12, 13, 14, 15, 16, 17,
-         18, 19, 20, 21, 22, 23, 24, 25)
+A_TICK = (2, 3, 5, 7, 9, 11, 14, 18)
+I_TICK = (4, 8, 11, 15)
+C_TICK = (8, 10, 12, 13, 16, 17, 19, 20, 21, 22, 23, 24, 25, 26, 27, 28)
 AHEAD = 3
 LAG_CORE = 1
 LAG_Y1 = 4

time: 78.1 us -> 75.5 us (0.967)
  Pallas kernels: 76.4 us -> 73.7 us
    pallas_call x1, Pallas kernels: 76.4 us -> 73.7 us  [body(): pl.pallas_call(kernel, out_shape=jax.ShapeDtypeStruct((TILE, 1024), BF16)...]
where the time goes in v5:
time: 75.5 us; the launch traced here: 75.1 us
  Pallas kernels  73.7 us (98%)
  local copies, waits for them, and re-layouts  1.4 us (2%)
    pallas_call x1, Pallas kernels, body(): pl.pallas_call(kernel, out_shape=jax.ShapeDtypeStruct((TILE, 1024), BF16)...  73.7 us

profile of v5, /device:TPU:32, one launch (start us, length us, event | category | flops | bytes accessed | tf_op | source)
XLA Modules:
  0.0 75.1 jit_solution(4340868415484240262)
XLA Ops:
  0.0 0.0 copy-start
  0.0 0.7 copy-done
  0.7 73.7 %shard_map.37 = bf16[128,1024]{1,0:T(8,128)(2,1)S(1)} custom-call(bf16[2048,512]{1,0:T(8,128)(2,1)} %integrals.1, bf16[512,1024]{1,0:T(8,128)(2,1)} %amplitudes.1, s32[16,64]{1,0:T(8,128)S(1)} %copy-done), custom_call_target="tpu_custom_call" | custom-call | flops 2147483648 | bytes 4194304 | tf_op jit(solution)/shard_map/pallas_call | solution.py:301
  74.4 0.7 copy.5
Async XLA Ops:
  0.0 0.7 copy-start

commit v6 on v5

--- a/solution.py
+++ b/solution.py
@@ -240,6 +240,17 @@
                 core_copy(c).start()
                 product(c, u, w, core, keep)
 
+        @pl.when(t == C_TICK[-1] + 2)
+        def _():
+            for n in range(4):
+                i_own(n, True)
+                i_forward(n, True)
+            for d in range(2):
+                for q in range(NQ):
+                    a_own(q, d).wait_send()
+                    a_pass(q, d).wait_send()
+            remote(give, give, c_send, c_recv.at[0], other_core).wait_send()
+
         c1 = table(t - LAG_CORE, C_TICK, range(NC), -1)
 
         @pl.when(c1 >= 0)
@@ -285,14 +296,7 @@
 
     lax.fori_loop(0, C_TICK[-1] + LAG_Y2 + 1, tick, 0)
 
-    for u in range(4):
-        i_own(u, True)
-        i_forward(u, True)
-    for d in range(2):
-        for q in range(NQ):
-            a_own(q, d).wait_send()
-            a_pass(q, d).wait_send()
-    for buf, sem in ((give, c_send), (y1, y1_send), (y2, y2_send), (zgot, z_send)):
+    for buf, sem in ((y1, y1_send), (y2, y2_send), (zgot, z_send)):
         remote(buf, buf, sem, c_recv.at[0], other_core).wait_send()
 
 

time: 75.5 us -> 75.6 us (level)
  no operation moved by 1% of the time
where the time goes in v6:
time: 75.6 us; the launch traced here: 74.7 us
  Pallas kernels  73.3 us (97%)
  local copies, waits for them, and re-layouts  1.4 us (2%)
    pallas_call x1, Pallas kernels, body(): pl.pallas_call(kernel, out_shape=jax.ShapeDtypeStruct((TILE, 1024), BF16)...  73.3 us

profile of v6, /device:TPU:32, one launch (start us, length us, event | category | flops | bytes accessed | tf_op | source)
XLA Modules:
  0.0 74.7 jit_solution(18124614774896522931)
XLA Ops:
  0.0 0.0 copy-start
  0.0 0.7 copy-done
  0.7 73.3 %shard_map.37 = bf16[128,1024]{1,0:T(8,128)(2,1)S(1)} custom-call(bf16[2048,512]{1,0:T(8,128)(2,1)} %integrals.1, bf16[512,1024]{1,0:T(8,128)(2,1)} %amplitudes.1, s32[16,64]{1,0:T(8,128)S(1)} %copy-done), custom_call_target="tpu_custom_call" | custom-call | flops 2147483648 | bytes 4194304 | tf_op jit(solution)/shard_map/pallas_call | solution.py:305
  74.0 0.7 copy.5
Async XLA Ops:
  0.0 0.7 copy-start
